TPU v7x, 32 devices: a whole 2x2x4 slice. The times are simulated.
32 devices in a mesh: gx: 8 (over y, x, core), gy: 4 (over z).
Axes of the slice: x: 2, y: 2, z: 4, core: 2. Of those that a mesh axis runs over, the one named last changes fastest.
Arguments:
- leaf_load: bfloat16 [65536, 384], P(('gx', 'gy')), may hold values from -6 to 6
- front_zero: bfloat16 [65536, 8192], P(('gx', 'gy')), may hold values from -0.046875 to 0.046875
- front_one: bfloat16 [32768, 8192], P(('gx', 'gy')), may hold values from -0.046875 to 0.046875
- front_two: bfloat16 [16384, 8192], P(('gx', 'gy')), may hold values from -0.046875 to 0.046875
- front_root: bfloat16 [8192, 8192], P(('gx', 'gy')), may hold values from -0.046875 to 0.046875
- load_one: float32 [32768, 384], P(('gx', 'gy')), may hold values from -6 to 6
- load_two: float32 [16384, 384], P(('gx', 'gy')), may hold values from -6 to 6
- load_root: float32 [8192, 384], P(('gx', 'gy')), may hold values from -6 to 6
- map_one: int32 [8192, 2], replicated, may hold values from 0 to 2047
- map_two: int32 [8192, 2], replicated, may hold values from 0 to 1023
- map_root: int32 [8192, 2], replicated, may hold values from 0 to 511
- adjoint: float32 [128, 64, 384], P('gx', 'gy'), may hold values from -6 to 6
Outputs:
- root_solution: float32 [8192, 384], P(('gx', 'gy'))
- gradient: float32 [128, 64, 384], P('gx', 'gy')
All inputs are finite; a program needn't handle non-finite values.
Results may differ from a plain program's by a relative error of at most 0.0055.
Values may be sent and summed in bfloat16 or wider, within the bound.
A program may use at most 128 MiB of HBM per device.

v0:
```python
import jax
import jax.numpy as jnp
from jax import lax
from jax.sharding import PartitionSpec as P


def swapped(x, axis, distance):
    return lax.ppermute(x, axis, [(i, i ^ 1 << distance) for i in range(lax.axis_size(axis))])


def padded_2(cells, sides, width):
    for axis, dim in sides:
        count = lax.axis_size(axis)
        ends = count - 1
        head = lax.slice_in_dim(cells, 0, width, axis=dim)
        tail = lax.slice_in_dim(cells, cells.shape[dim] - width, cells.shape[dim], axis=dim)
        cells = jnp.concatenate(
            [
                lax.ppermute(tail, axis, [(i, (i + 1) % count) for i in range(ends)]),
                cells,
                lax.ppermute(head, axis, [((i + 1) % count, i) for i in range(ends)]),
            ],
            axis=dim,
        )
    return cells


def group_rows(values, bits):
    values = lax.all_gather(values, "gy", axis=0, tiled=True)
    column = lax.axis_index("gx")
    for bit in range(bits):
        other = swapped(values, "gx", bit)
        upper = column >> bit & 1 == 1
        values = jnp.where(
            upper, jnp.concatenate([other, values], 0), jnp.concatenate([values, other], 0)
        )
    return values


def local(
    leaf_load,
    front_zero,
    front_one,
    front_two,
    front_root,
    load_one,
    load_two,
    load_root,
    map_one,
    map_two,
    map_root,
    adjoint,
):
    leaf_bits = lax.axis_size("gx").bit_length() - 4
    fronts = (front_zero, front_one, front_two)
    loads = (load_one, load_two, load_root)
    mappings = (map_one, map_two, map_root)
    column = lax.axis_index("gx")
    row_index = lax.axis_index("gy")
    state = leaf_load
    for level in range(3):
        bits = leaf_bits + level
        whole = group_rows(state, bits)
        product = jnp.dot(fronts[level], whole, preferred_element_type=jnp.float32)
        other = swapped(product, "gx", bits)
        upper = column >> bits & 1 == 1
        first = jnp.where(upper, other, product)
        second = jnp.where(upper, product, other)
        half = product.shape[0] // 2
        position = column % 2 ** (bits + 1) * lax.axis_size("gy") + row_index
        local_map = lax.dynamic_slice_in_dim(mappings[level], position * half, half, 0)
        total = (
            loads[level]
            + jnp.take(first, local_map[:, 0], axis=0)
            + jnp.take(second, local_map[:, 1], axis=0)
        )
        state = total.astype(jnp.bfloat16)
    whole = group_rows(state, leaf_bits + 3)
    root_solution = jnp.dot(front_root, whole, preferred_element_type=jnp.float32)
    cells_x = adjoint.shape[0]
    cells_y = adjoint.shape[1]
    width = adjoint.shape[2]
    plane = root_solution.reshape(cells_x, cells_y, width)
    stacked = jnp.stack([plane, adjoint])
    padded = padded_2(stacked, (("gx", 1), ("gy", 2)), 1)
    padded_u = padded[0]
    padded_a = padded[1]
    gradient = jnp.zeros((cells_x, cells_y, width), jnp.float32)
    for lo_x, lo_y in ((2, 1), (0, 1), (1, 2), (1, 0)):
        near_u = padded_u[lo_x : lo_x + cells_x, lo_y : lo_y + cells_y]
        near_a = padded_a[lo_x : lo_x + cells_x, lo_y : lo_y + cells_y]
        gradient = gradient + (plane - near_u) * (adjoint - near_a)
    return (root_solution, gradient)


def solution(mesh):
    in_specs = (
        P(("gx", "gy"), None),
        P(("gx", "gy"), None),
        P(("gx", "gy"), None),
        P(("gx", "gy"), None),
        P(("gx", "gy"), None),
        P(("gx", "gy"), None),
        P(("gx", "gy"), None),
        P(("gx", "gy"), None),
        P(),
        P(),
        P(),
        P("gx", "gy", None),
    )
    out_specs = (P(("gx", "gy"), None), P("gx", "gy", None))
    return jax.shard_map(local, mesh=mesh, in_specs=in_specs, out_specs=out_specs, check_vma=False)
```

profile of v0, /device:TPU:12, one launch (start us, length us, event | category | flops | bytes accessed | tf_op | source)
XLA Modules:
  0.0 609.5 jit_solution(13438335921112895353)
XLA Ops:
  7.9 115.4 %all-gather.4.cloned.1.call-done = bf16[8192,384]{1,0:T(8,128)(2,1)} async-done(((bf16[2048,384]{1,0:T(8,128)(2,1)}), bf16[8192,384]{1,0:T(8,128)(2,1)}) %all-gather.4.cloned.1.call-update) | async-done | bytes 6291472 | tf_op jit(solution)/shard_map/all_gather | solution.py:29
  123.3 22.0 %fusion.38 = f32[2048,384]{1,0:T(8,128)S(1)} fusion(bf16[2048,8192]{1,0:T(8,128)(2,1)} %param.19, bf16[8192,384]{1,0:T(8,128)(2,1)} %all-gather.4.cloned.1.call-done), kind=kOutput, calls=%fused_computation.98 | convolution fusion | flops 12884901888 | bytes 42991616 | tf_op jit(solution)/shard_map/dot_general | solution.py:64
  147.0 4.2 collective-permute-done
  151.2 4.9 broadcast_select_fusion.1
  156.1 6.9 %gather_fusion.1 = f32[1024,384]{1,0:T(8,128)} fusion(f32[2048,384]{1,0:T(8,128)} %get-tuple-element.6, s32[1024]{0:T(1024)S(1)} %fusion.34), kind=kCustom, calls=%fused_computation.3.clone | custom fusion | bytes 3149824 | tf_op jit(solution)/shard_map/jit(_take)/gather | solution.py:75
  162.9 4.8 gather_fusion
  167.7 3.4 fusion.21
  171.3 62.3 %all-gather.6.cloned.1.call-done = bf16[4096,384]{1,0:T(8,128)(2,1)} async-done(((bf16[1024,384]{1,0:T(8,128)(2,1)}), bf16[4096,384]{1,0:T(8,128)(2,1)}) %all-gather.6.cloned.1.call-update) | async-done | bytes 3145744 | tf_op jit(solution)/shard_map/all_gather | solution.py:29
  233.5 6.0 collective-permute-done.1
  239.5 16.1 %fusion.22 = f32[1024,384]{0,1:T(8,128)S(1)} fusion(bf16[1024,8192]{1,0:T(8,128)(2,1)} %param.20, bf16[4096,384]{1,0:T(8,128)(2,1)} %all-gather.6.cloned.1.call-done, bf16[4096,384]{1,0:T(8,128)(2,1)} %collective-permute-done.1, pred[]{:T(512)S(6)} %eq.21), kind=kOutput, calls=%fused_computation.38 | convolution fusion | flops 6470762496 | bytes 24641536 | tf_op jit(solution)/shard_map/dot_general | solution.py:64
  258.1 34.2 %collective-permute-done.2 = f32[1024,384]{0,1:T(8,128)} collective-permute-done((f32[1024,384]{0,1:T(8,128)S(1)}, f32[1024,384]{0,1:T(8,128)}, u32[]{:S(2)}, u32[]{:S(2)}) %collective-permute-start.2) | collective-permute-done | bytes 1572896 | tf_op jit(solution)/shard_map/ppermute | solution.py:8
  292.3 2.9 broadcast_select_fusion.3
  303.7 37.2 %all-gather.8.cloned.1.call-done = bf16[2048,384]{1,0:T(8,128)(2,1)} async-done(((bf16[512,384]{1,0:T(8,128)(2,1)}), bf16[2048,384]{1,0:T(8,128)(2,1)}) %all-gather.8.cloned.1.call-update) | async-done | bytes 1572880 | tf_op jit(solution)/shard_map/all_gather | solution.py:29
  340.9 3.6 collective-permute-done.3
  348.7 68.8 %collective-permute-done.4 = bf16[4096,384]{1,0:T(8,128)(2,1)} collective-permute-done((bf16[4096,384]{1,0:T(8,128)(2,1)S(1)}, bf16[4096,384]{1,0:T(8,128)(2,1)}, u32[]{:S(2)}, u32[]{:S(2)}) %collective-permute-start.4) | collective-permute-done | bytes 3145760 | tf_op jit(solution)/shard_map/ppermute | solution.py:8
  417.5 8.9 %fusion.23 = f32[512,384]{0,1:T(8,128)S(1)} fusion(bf16[512,8192]{1,0:T(8,128)(2,1)} %param.21, bf16[4096,384]{1,0:T(8,128)(2,1)S(1)} %maximum_select_fusion.6, bf16[4096,384]{1,0:T(8,128)(2,1)} %collective-permute-done.4, pred[]{:T(512)S(6)} %eq.20), kind=kOutput, calls=%fused_computation.40 | convolution fusion | flops 3249537024 | bytes 15466497 | tf_op jit(solution)/shard_map/dot_general | solution.py:64
  427.8 17.3 %collective-permute-done.5 = f32[512,384]{0,1:T(8,128)S(1)} collective-permute-done((f32[512,384]{0,1:T(8,128)S(1)}, f32[512,384]{0,1:T(8,128)S(1)}, u32[]{:S(2)}, u32[]{:S(2)}) %collective-permute-start.5) | collective-permute-done | bytes 786464 | tf_op jit(solution)/shard_map/ppermute | solution.py:8
  448.1 17.2 %all_gather.15 = bf16[1024,384]{1,0:T(8,128)(2,1)S(1)} all-gather(bf16[256,384]{1,0:T(8,128)(2,1)S(1)} %fusion.32), channel_id=1, replica_groups=mesh['gx'=8,'gy'=4] {'gy'}, dimensions={0}, use_global_device_ids=true | all-gather | bytes 983040 | tf_op jit(solution)/shard_map/all_gather | solution.py:29
  469.5 35.0 %collective-permute-done.7 = bf16[2048,384]{1,0:T(8,128)(2,1)S(1)} collective-permute-done((bf16[2048,384]{1,0:T(8,128)(2,1)S(1)}, bf16[2048,384]{1,0:T(8,128)(2,1)S(1)}, u32[]{:S(2)}, u32[]{:S(2)}) %collective-permute-start.7) | collective-permute-done | bytes 1572896 | tf_op jit(solution)/shard_map/ppermute | solution.py:8
  504.5 7.2 %maximum_select_fusion.7 = bf16[4096,384]{1,0:T(8,128)(2,1)S(1)} fusion(bf16[2048,384]{1,0:T(8,128)(2,1)S(1)} %maximum_select_fusion.8, bf16[2048,384]{1,0:T(8,128)(2,1)S(1)} %collective-permute-done.7, pred[]{:T(512)S(6)} %eq.20), kind=kLoop, calls=%fused_computation.31 | loop fusion | flops 14155776 | bytes 6291457 | tf_op jit(solution)/shard_map/jit(_where)/select_n | solution.py:34
  512.3 68.8 %collective-permute-done.8 = bf16[4096,384]{1,0:T(8,128)(2,1)S(1)} collective-permute-done((bf16[4096,384]{1,0:T(8,128)(2,1)S(1)}, bf16[4096,384]{1,0:T(8,128)(2,1)S(1)}, u32[]{:S(2)}, u32[]{:S(2)}) %collective-permute-start.8) | collective-permute-done | bytes 3145760 | tf_op jit(solution)/shard_map/ppermute | solution.py:8
  587.9 3.9 collective-permute-done.9
  591.8 3.8 collective-permute-start.12
  597.9 3.8 collective-permute-done.11
  (67 shorter events, 37.2 us)
Async XLA Ops:
  7.2 116.2 %all-gather.4.cloned.1.call-start = ((), (), s32[]{:S(2)}) async-start(), calls=%async_computation | async-start | bytes 7864320 | tf_op jit(solution)/shard_map/all_gather | solution.py:29
  7.9 225.6 %all-gather.6.cloned.1.call-start = ((), (), s32[]{:S(2)}) async-start(), calls=%async_computation.1 | async-start | bytes 3932160 | tf_op jit(solution)/shard_map/all_gather | solution.py:29
  145.3 1.7 copy-start.2
  145.3 5.9 collective-permute-start
  171.2 169.7 %all-gather.8.cloned.1.call-start = ((), (), s32[]{:S(2)}) async-start(), calls=%async_computation.2 | async-start | bytes 1966080 | tf_op jit(solution)/shard_map/all_gather | solution.py:29
  233.5 6.0 collective-permute-start.1
  255.7 36.6 %collective-permute-start.2 = (f32[1024,384]{0,1:T(8,128)S(1)}, f32[1024,384]{0,1:T(8,128)}, u32[]{:S(2)}, u32[]{:S(2)}) collective-permute-start(f32[1024,384]{0,1:T(8,128)S(1)} %fusion.22), channel_id=1, source_target_pairs={{0,8},{4,12},{8,0},{12,4},{16,24},{20,28},{24,16},{28,20},{1,9},{5... | collective-permute-start | bytes 4718600 | tf_op jit(solution)/shard_map/ppermute | solution.py:8
  299.8 1.8 copy-start.3
  340.9 3.6 collective-permute-start.3
  347.1 70.3 %collective-permute-start.4 = (bf16[4096,384]{1,0:T(8,128)(2,1)S(1)}, bf16[4096,384]{1,0:T(8,128)(2,1)}, u32[]{:S(2)}, u32[]{:S(2)}) collective-permute-start(bf16[4096,384]{1,0:T(8,128)(2,1)S(1)} %maximum_select_fusion.6), channel_id=1, source_target_pairs={{0,8},{4,12},{8,0},{12,4},{16,24},{20,28},{24,16},{28,20},{1,9},{5... | collective-permute-start | bytes 9437192 | tf_op jit(solution)/shard_map/ppermute | solution.py:8
  426.3 18.8 %collective-permute-start.5 = (f32[512,384]{0,1:T(8,128)S(1)}, f32[512,384]{0,1:T(8,128)S(1)}, u32[]{:S(2)}, u32[]{:S(2)}) collective-permute-start(f32[512,384]{0,1:T(8,128)S(1)} %fusion.23), channel_id=1, source_target_pairs={{0,16},{4,20},{8,24},{12,28},{16,0},{20,4},{24,8},{28,12},{1,17},{... | collective-permute-start | bytes 2359304 | tf_op jit(solution)/shard_map/ppermute | solution.py:8
  445.9 2.0 copy-start.4
  465.3 2.3 collective-permute-start.6
  468.0 113.1 %copy-start.5 = (bf16[256,8192]{1,0:T(8,128)(2,1)S(1)}, bf16[256,8192]{1,0:T(8,128)(2,1)}, u32[]{:S(2)}) copy-start(bf16[256,8192]{1,0:T(8,128)(2,1)} %param.22) | copy-start | bytes 12582916
  468.0 36.5 %collective-permute-start.7 = (bf16[2048,384]{1,0:T(8,128)(2,1)S(1)}, bf16[2048,384]{1,0:T(8,128)(2,1)S(1)}, u32[]{:S(2)}, u32[]{:S(2)}) collective-permute-start(bf16[2048,384]{1,0:T(8,128)(2,1)S(1)} %maximum_select_fusion.8), channel_id=1, source_target_pairs={{0,8},{4,12},{8,0},{12,4},{16,24},{20,28},{24,16},{28,20},{1,9},{5... | collective-permute-start | bytes 4718600 | tf_op jit(solution)/shard_map/ppermute | solution.py:8
  511.7 71.8 %copy-start = (f32[16,16,384]{2,1,0:T(8,128)S(1)}, f32[16,16,384]{2,1,0:T(8,128)}, u32[]{:S(2)}) copy-start(f32[16,16,384]{2,1,0:T(8,128)} %param.29) | copy-start | bytes 1179652
  511.7 69.4 %collective-permute-start.8 = (bf16[4096,384]{1,0:T(8,128)(2,1)S(1)}, bf16[4096,384]{1,0:T(8,128)(2,1)S(1)}, u32[]{:S(2)}, u32[]{:S(2)}) collective-permute-start(bf16[4096,384]{1,0:T(8,128)(2,1)S(1)} %maximum_select_fusion.7), channel_id=1, source_target_pairs={{0,16},{4,20},{8,24},{12,28},{16,0},{20,4},{24,8},{28,12},{1,17},{... | collective-permute-start | bytes 9437192 | tf_op jit(solution)/shard_map/ppermute | solution.py:8
  583.5 18.5 %copy-start.1 = (f32[384,256]{0,1:T(8,128)}, f32[384,256]{0,1:T(8,128)S(1)}, u32[]{:S(2)}) copy-start(f32[384,256]{0,1:T(8,128)S(1)} %fusion.12) | copy-start | bytes 1179652
  583.5 4.3 collective-permute-start.10
  585.4 6.3 %collective-permute-start.9 = (f32[2,1,16,384]{3,2,1,0:T(8,128)S(1)}, f32[2,1,16,384]{3,2,1,0:T(8,128)S(1)}, u32[]{:S(2)}, u32[]{:S(2)}) collective-permute-start(f32[2,1,16,384]{3,2,1,0:T(8,128)S(1)} %get-tuple-element.15), channel_id=1, source_target_pairs={{0,4},{4,8},{8,12},{12,16},{16,20},{20,24},{24,28},{1,5},{5,9},{9,... | collective-permute-start | bytes 147464 | tf_op jit(solution)/shard_map/ppermute | solution.py:19
  591.8 6.0 collective-permute-start.12
  595.6 6.0 collective-permute-start.11
Sparse Core Ops, SparseCore 0:
  9.6 113.7 all-gather.3
  171.3 62.1 all-gather.5
  303.8 37.0 all-gather.7
where the time goes:
time: 610 us
  waiting for transfers between devices  463 us (76%)
  matrix products  49.3 us (8%)
  other arithmetic  25.4 us (4%)
  local copies, waits for them, and re-layouts  23.9 us (4%)
  blocking collectives  17.2 us (3%)
  starting transfers between devices  16.2 us (3%)
  between operations  14.1 us (2%)
    ppermute x9, waiting for transfers between devices, swapped(): lax.ppermute(x, axis, [(i, i ^ 1 << distance) for i in range(lax.axis_siz...  240 us
    all_gather x3, waiting for transfers between devices, group_rows(): values = lax.all_gather(values, 'gy', axis=0, tiled=True)  215 us
    dot_general x3, matrix products, local(): product = jnp.dot(fronts[level], whole, preferred_element_type=jnp.float32)  47 us
    all_gather x1, blocking collectives, group_rows(): values = lax.all_gather(values, 'gy', axis=0, tiled=True)  17.2 us
  transfers between devices with their start and end apart: 16, of which 15 were waited for; matrix products, arithmetic and copies ran while one was open for 0% of the time, Pallas kernels for 0%

commit v1 on v0

v1 whole, which is shorter than its diff:
```python
import functools

import jax
import jax.numpy as jnp
from jax import lax
from jax.experimental import pallas as pl
from jax.experimental.pallas import tpu as pltpu
from jax.sharding import PartitionSpec as P

MESH = pl.DeviceIdType.MESH
CHUNK = 128
LINK = 92e3
PAIR = 500e3


class Plan:
    def __init__(self):
        self.now = 0.0
        self.free = {}

    def send(self, link, size, rate):
        begin = max(self.now, self.free.get(link, 0.0))
        self.free[link] = begin + size / rate
        return self.free[link] + 1.0


def count_copies(n, leaf_bits, chunks):
    total = 0
    for level in range(4):
        bits = leaf_bits + level
        total += chunks * (2 * (n - 1) + bits * (2 * n - 1) + 2**bits + 1)
    return total


def kernel(
    n, gx, leaf_ref, f0, f1, f2, f3, l1, l2, l3, p1, p2, p3, out_ref,
    z0, z1, z2, z3, s1, s2, s3, r1, r2, r3, k1, k2, k3, w_ref, a_ref, a_sem, send_sems, recv_sems,
):
    fronts, loads, picks = (f0, f1, f2, f3), (l1, l2, l3), (p1, p2, p3)
    zs, sends, recvs, keeps = (z0, z1, z2, z3), (s1, s2, s3), (r1, r2, r3), (k1, k2, k3)
    gx_bits = gx.bit_length() - 1
    leaf_bits = gx_bits - 3
    chunks = out_ref.shape[1] // CHUNK
    column, line = lax.axis_index("gx"), lax.axis_index("gy")
    digit = [(column // 2**b) % 2 for b in range(gx_bits)]
    partner = [column + (1 - 2 * digit[b]) * 2**b for b in range(gx_bits)]
    plan = Plan()
    used = [0]
    open_sends = []

    barrier = pltpu.get_barrier_semaphore()
    for b in range(gx_bits):
        pl.semaphore_signal(barrier, inc=1, device_id={"gx": partner[b]}, device_id_type=MESH)

    @pl.when(line > 0)
    def _():
        pl.semaphore_signal(barrier, inc=1, device_id={"gy": line - 1}, device_id_type=MESH)

    @pl.when(line < n - 1)
    def _():
        pl.semaphore_signal(barrier, inc=1, device_id={"gy": line + 1}, device_id_type=MESH)

    neighbours = jnp.minimum(line, 1) + jnp.minimum(n - 1 - line, 1)
    pl.semaphore_wait(barrier, gx_bits + neighbours)

    def guarded(cond, act):
        if cond is None:
            act()
        else:
            pl.when(cond)(act)

    def transfer(src, dst, target, cond=None, recv_cond=None):
        slot = used[0]
        used[0] += 1

        def make():
            return pltpu.make_async_remote_copy(
                src_ref=src, dst_ref=dst, send_sem=send_sems.at[slot], recv_sem=recv_sems.at[slot],
                device_id=target, device_id_type=MESH,
            )

        guarded(cond, lambda: make().start())
        open_sends.append((cond, lambda: make().wait_send()))
        return lambda: guarded(recv_cond, lambda: make().wait_recv())

    parity = [0]

    def tile_rows(level):
        return min(256, fronts[level].shape[0])

    def tile_copy(level, tile, slot):
        rows = tile_rows(level)
        return pltpu.make_async_copy(
            fronts[level].at[pl.ds(pl.multiple_of(tile * rows, rows), rows), :],
            a_ref.at[slot, pl.ds(0, rows), :],
            a_sem.at[slot],
        )

    def matmul(level, chunk):
        rows = tile_rows(level)
        tiles = fronts[level].shape[0] // rows
        base = parity[0]
        parity[0] = (base + tiles) % 2
        tile_copy(level, 0, base).start()

        def body(tile, _):
            slot = (base + tile) % 2

            @pl.when(tile + 1 < tiles)
            def _():
                tile_copy(level, tile + 1, (base + tile + 1) % 2).start()

            tile_copy(level, tile, slot).wait()
            product = jnp.dot(
                a_ref[slot, :rows, :], zs[level][chunk], preferred_element_type=jnp.float32
            )
            at = pl.ds(pl.multiple_of(tile * rows, rows), rows)
            if level < 3:
                high = product.astype(jnp.bfloat16)
                low = (product - high.astype(jnp.float32)).astype(jnp.bfloat16)
                w_ref[at, :CHUNK] = high
                w_ref[at, CHUNK:] = low
            else:
                out_ref[at, chunk * CHUNK : (chunk + 1) * CHUNK] = product
            return 0

        lax.fori_loop(0, tiles, body, 0)
        plan.now += tiles * rows / 256 * 1.3 + 1.0

    def pick(level, chunk):
        depth = fronts[level].shape[0]
        half = depth // 2
        rows = min(256, half)
        tiles = half // rows
        cols = pl.ds(chunk * CHUNK, CHUNK)

        def chosen(at, width):
            lanes = lax.broadcasted_iota(jnp.int32, (rows, depth), 1)
            hot = jnp.where(lanes == picks[level][at, :], 1.0, 0.0).astype(jnp.bfloat16)
            return jnp.dot(hot, w_ref[:depth, :width], preferred_element_type=jnp.float32)

        def outgoing(tile, _):
            at = pl.ds(pl.multiple_of(half + tile * rows, rows), rows)
            to = pl.ds(pl.multiple_of(tile * rows, rows), rows)
            sends[level][chunk, to, :] = chosen(at, CHUNK).astype(jnp.bfloat16)
            return 0

        def staying(tile, _):
            at = pl.ds(pl.multiple_of(tile * rows, rows), rows)
            both = chosen(at, 2 * CHUNK)
            keeps[level][chunk, at, :] = loads[level][at, cols] + (
                both[:, :CHUNK] + both[:, CHUNK:]
            )
            return 0

        lax.fori_loop(0, tiles, outgoing, 0)
        plan.now += tiles * 0.5 * depth / 2048
        b = leaf_bits + level
        landed = transfer(
            sends[level].at[chunk], recvs[level].at[chunk], {"gx": partner[b]}
        )
        size = half * CHUNK * 2
        ready = plan.send(b, size * (1 if b == 0 else 2), PAIR if b == 0 else LINK)
        lax.fori_loop(0, tiles, staying, 0)
        plan.now += tiles * 0.6 * depth / 2048
        return landed, ready

    def stream(chunk):
        cols = pl.ds(chunk * CHUNK, CHUNK)
        for level in range(4):
            rows = fronts[level].shape[0]
            bits = leaf_bits + level
            order = list(range(1, bits)) + ([0] if bits else [])
            buf = zs[level]
            size = rows * CHUNK * 2
            group = column % 2**bits

            def shard(index, block=None):
                block = group if block is None else block
                start = (block * n + index) * rows
                return buf.at[chunk, pl.ds(pl.multiple_of(start, rows), rows), :]

            def span(block):
                start = block * n * rows
                return buf.at[chunk, pl.ds(pl.multiple_of(start, rows), n * rows), :]

            def flipped(mask):
                block = group
                for b in range(bits):
                    if mask >> b & 1:
                        block = block + (1 - 2 * digit[b]) * 2**b
                return block

            if level == 0:
                own = pl.ds(pl.multiple_of((group * n + line) * rows, rows), rows)
                buf[chunk, own, :] = leaf_ref[:, cols]
            across = {b: [] for b in order}
            arrive = {b: 0.0 for b in order}

            def share(index, cond):
                for b in order:
                    across[b].append(
                        transfer(shard(index), shard(index), {"gx": partner[b]}, cond, cond)
                    )
                    arrive[b] = plan.send(
                        b, size * (1 if b == 0 else 2), PAIR if b == 0 else LINK
                    )

            def forward(step):
                up = transfer(
                    shard(line - step + 1), shard(line - step + 1), {"gy": line + 1},
                    (line - step + 1 >= 0) & (line < n - 1), line >= step,
                )
                down = transfer(
                    shard(line + step - 1), shard(line + step - 1), {"gy": line - 1},
                    (line + step - 1 < n) & (line > 0), line + step < n,
                )
                return up, down, plan.send("z", 2 * size, LINK)

            up, down, ready = forward(1)
            share(line, None)
            for step in range(1, n):
                yield ready
                up()
                down()
                if step < n - 1:
                    up, down, ready = forward(step + 1)
                share(line - step, line >= step)
                share(line + step, line + step < n)
            pending = {1 << b: (across[b], arrive[b], at) for at, b in enumerate(order)}
            while pending:
                mask = min(pending, key=lambda m: (pending[m][1], m))
                waits, ready, at = pending.pop(mask)
                yield ready
                for wait in waits:
                    wait()
                for later in range(at + 1, len(order)):
                    b = order[later]
                    got = transfer(
                        span(flipped(mask)), span(flipped(mask)), {"gx": partner[b]}
                    )
                    when = plan.send(
                        b, n * size * (1 if b == 0 else 2), PAIR if b == 0 else LINK
                    )
                    pending[mask | 1 << b] = ([got], when, later)
            matmul(level, chunk)
            if level < 3:
                yield plan.now
                landed, ready = pick(level, chunk)
                yield ready
                landed()
                rows = rows // 2
                group = column % 2 ** (bits + 1)
                own = pl.ds(pl.multiple_of((group * n + line) * rows, rows), rows)
                zs[level + 1][chunk, own, :] = (
                    keeps[level][chunk] + recvs[level][chunk].astype(jnp.float32)
                ).astype(jnp.bfloat16)

    lead = 2 * leaf_ref.shape[0] * CHUNK * 2 / LINK
    waiting = []
    for chunk in range(chunks):
        waiting.append([0.0 if chunk < 2 else 3.5 * lead, chunk, stream(chunk)])
    while waiting:
        entry = min(waiting, key=lambda e: (e[0], e[1]))
        plan.now = max(plan.now, entry[0])
        try:
            entry[0] = next(entry[2])
        except StopIteration:
            waiting.remove(entry)
    for cond, wait in open_sends:
        guarded(cond, wait)


def halos(cells):
    sides = []
    for axis, dim in (("gx", 0), ("gy", 1)):
        count = lax.axis_size(axis)
        head = lax.slice_in_dim(cells, 0, 1, axis=dim)
        tail = lax.slice_in_dim(cells, cells.shape[dim] - 1, cells.shape[dim], axis=dim)
        sides.append(lax.ppermute(tail, axis, [(i, i + 1) for i in range(count - 1)]))
        sides.append(lax.ppermute(head, axis, [(i + 1, i) for i in range(count - 1)]))
    return sides


def local(
    leaf_load, front_zero, front_one, front_two, front_root, load_one, load_two, load_root,
    map_one, map_two, map_root, adjoint,
):
    gx, n = lax.axis_size("gx"), lax.axis_size("gy")
    leaf_bits = gx.bit_length() - 4
    column, line = lax.axis_index("gx"), lax.axis_index("gy")
    rows0, cases = leaf_load.shape
    chunks = cases // CHUNK
    front = front_zero.shape[1]
    picks = []
    for level, mapping in enumerate((map_one, map_two, map_root)):
        bits = leaf_bits + level
        half = rows0 >> level + 1
        upper = column >> bits & 1
        rows = []
        for owner in (column, column ^ 1 << bits):
            position = owner % 2 ** (bits + 1) * n + line
            rows.append(lax.dynamic_slice(mapping, (position * half, upper), (half, 1)))
        picks.append(jnp.concatenate(rows, 0))
    vmem = pl.BlockSpec(memory_space=pltpu.VMEM)
    hbm = pl.BlockSpec(memory_space=pl.ANY)
    halves = [rows0 >> k for k in (1, 2, 3)]
    copies = count_copies(n, leaf_bits, chunks)
    root_solution = pl.pallas_call(
        functools.partial(kernel, n, gx),
        out_shape=jax.ShapeDtypeStruct((rows0 // 8, cases), jnp.float32),
        in_specs=[vmem] + [hbm] * 4 + [vmem] * 6,
        out_specs=vmem,
        scratch_shapes=[pltpu.VMEM((chunks, front, CHUNK), jnp.bfloat16)] * 4
        + [pltpu.VMEM((chunks, half, CHUNK), jnp.bfloat16) for half in halves] * 2
        + [pltpu.VMEM((chunks, half, CHUNK), jnp.float32) for half in halves]
        + [
            pltpu.VMEM((rows0, 2 * CHUNK), jnp.bfloat16),
            pltpu.VMEM((2, min(256, rows0), front), jnp.bfloat16),
            pltpu.SemaphoreType.DMA((2,)),
            pltpu.SemaphoreType.DMA((copies,)),
            pltpu.SemaphoreType.DMA((copies,)),
        ],
        compiler_params=pltpu.CompilerParams(
            collective_id=0, has_side_effects=True, vmem_limit_bytes=60 * 2**20
        ),
        cost_estimate=pl.CostEstimate(
            flops=30 * rows0 // 8 * front * cases, bytes_accessed=180_000_000, transcendentals=0
        ),
    )(leaf_load, front_zero, front_one, front_two, front_root, load_one, load_two, load_root, *picks)
    plane = root_solution.reshape(adjoint.shape)
    near_a = halos(adjoint)
    near_u = halos(plane)

    def moved(cells, sides):
        return (
            jnp.concatenate([sides[0], cells[:-1]], 0),
            jnp.concatenate([cells[1:], sides[1]], 0),
            jnp.concatenate([sides[2], cells[:, :-1]], 1),
            jnp.concatenate([cells[:, 1:], sides[3]], 1),
        )

    gradient = jnp.zeros_like(plane)
    for u, a in zip(moved(plane, near_u), moved(adjoint, near_a)):
        gradient = gradient + (plane - u) * (adjoint - a)
    return root_solution, gradient


def solution(mesh):
    rows = P(("gx", "gy"), None)
    cells = P("gx", "gy", None)
    return jax.shard_map(
        local,
        mesh=mesh,
        in_specs=(rows,) * 8 + (P(),) * 3 + (cells,),
        out_specs=(rows, cells),
        check_vma=False,
    )
```

time: 610 us -> 319 us (0.52)
  waiting for transfers between devices: 463 us -> 3.71 us
  Pallas kernels: 0 us -> 273 us
  matrix products: 49.3 us -> 0 us
  other arithmetic: 25.4 us -> 2.21 us
  blocking collectives: 17.2 us -> 0 us
  local copies, waits for them, and re-layouts: 23.9 us -> 10.7 us
  between operations: 14.1 us -> 0.94 us
  starting transfers between devices: 16.2 us -> 26.5 us
    pallas_call x0 -> x1, Pallas kernels: none -> 273 us  [local(): pl.pallas_call(functools.partial(kernel, n, gx), out_shape=jax.ShapeDtype...]
    ppermute x13 -> x8, waiting for transfers between devices: 248 us -> 3.71 us  [the longest x4 3.7 us: halos(): lax.ppermute(head, axis, [(i + 1, i) for i in range(count - 1)])]
    all_gather x3 -> x0, waiting for transfers between devices: 215 us -> none  [group_rows(): values = lax.all_gather(values, 'gy', axis=0, tiled=True)]
    dot_general x4 -> x0, matrix products: 49.3 us -> none  [the longest x3 47 us: local(): product = jnp.dot(fronts[level], whole, preferred_element_type=jnp.float32)]
    select_n x9 -> x0, other arithmetic: 18.2 us -> none  [the longest x3 10.3 us: group_rows(): jnp.where(upper, jnp.concatenate([other, values], 0), jnp.concatenate([va...]
    gather x6 -> x0, local copies, waits for them, and re-layouts: 17.7 us -> none  [the longest x3 10.2 us: local(): jnp.take(second, local_map[:, 1], axis=0)]
    all_gather x1 -> x0, blocking collectives: 17.2 us -> none  [group_rows(): values = lax.all_gather(values, 'gy', axis=0, tiled=True)]
    ppermute x13 -> x8, starting transfers between devices: 16.1 us -> 26.5 us  [the longest x4 14.6 us: halos(): lax.ppermute(head, axis, [(i + 1, i) for i in range(count - 1)])]
  transfers between devices with their start and end apart: 16 -> 8, of which waited for: 15 -> 1; matrix products, arithmetic and copies ran while one was open for 0% -> 1% of each run, Pallas kernels for 0% -> 0%
where the time goes in v1:
time: 319 us; the launch traced here: 317 us
  Pallas kernels  273 us (86%)
  starting transfers between devices  26.5 us (8%)
  local copies, waits for them, and re-layouts  10.7 us (3%)
  waiting for transfers between devices  3.71 us (1%)
    pallas_call x1, Pallas kernels, local(): pl.pallas_call(functools.partial(kernel, n, gx), out_shape=jax.ShapeDtype...  273 us
    ppermute x4, starting transfers between devices, halos(): lax.ppermute(head, axis, [(i + 1, i) for i in range(count - 1)])  14.6 us
    ppermute x4, starting transfers between devices, halos(): lax.ppermute(tail, axis, [(i, i + 1) for i in range(count - 1)])  11.9 us
  transfers between devices with their start and end apart: 8, of which 1 were waited for; matrix products, arithmetic and copies ran while one was open for 1% of the time, Pallas kernels for 0%

profile of v1, /device:TPU:12, one launch (start us, length us, event | category | flops | bytes accessed | tf_op | source)
XLA Modules:
  0.0 317.4 jit_solution(1341665811951119088)
XLA Ops:
  0.8 0.8 fusion.15
  1.5 1.1 copy.21.p2
  2.6 0.8 fusion.14
  3.4 0.9 copy.22.p3
  4.2 0.8 fusion.16
  5.0 1.4 copy.20.p1
  6.4 273.4 %shard_map.131 = f32[256,384]{1,0:T(8,128)} custom-call(bf16[2048,384]{1,0:T(8,128)(2,1)} %leaf_ref.1, bf16[2048,8192]{1,0:T(8,128)(2,1)} %f0.1, bf16[1024,8192]{1,0:T(8,128)(2,1)} %f1.1, bf16[512,8192]{1,0:T(8,128)(2,1)} %f2.1, bf16[256,8192]{1,0:T(8,128)(2,1)} %f3.1, f32[1024,384]{1,0:T(8,128)} %l1.1, f32[512,384]{1,0:T(8,128)} %l2.1, f32[256,384]{1,0:T(8,128)} %l3.1, ...), custom_call_target="tpu_custom_call" | custom-call | flops 24159191040 | bytes 180000000 | tf_op jit(solution)/shard_map/pallas_call | solution.py:309
  279.8 0.8 slice_bitcast_fusion
  280.6 2.5 collective-permute-start
  283.1 4.0 %collective-permute-start.2 = (f32[1,16,384]{2,1,0:T(8,128)S(1)}, f32[1,16,384]{2,1,0:T(8,128)S(1)}, u32[]{:S(2)}, u32[]{:S(2)}) collective-permute-start(f32[1,16,384]{2,1,0:T(8,128)S(1)} %get-tuple-element.16), channel_id=1, source_target_pairs={{4,0},{8,4},{12,8},{16,12},{20,16},{24,20},{28,24},{5,1},{9,5},{13... | collective-permute-start | bytes 73736 | tf_op jit(solution)/shard_map/ppermute | solution.py:281
  287.1 1.1 fusion.10
  288.1 3.6 %collective-permute-start.4 = (f32[16,1,384]{2,1,0:T(1,128)S(1)}, f32[16,1,384]{2,1,0:T(1,128)S(1)}, u32[]{:S(2)}, u32[]{:S(2)}) collective-permute-start(f32[16,1,384]{2,1,0:T(1,128)S(1)} %get-tuple-element.9), channel_id=1, source_target_pairs={{0,1},{1,2},{2,3},{4,5},{5,6},{6,7},{8,9},{9,10},{10,11},{12,13},{... | collective-permute-start | bytes 73736 | tf_op jit(solution)/shard_map/ppermute | solution.py:280
  291.7 4.1 %collective-permute-start.6 = (f32[16,1,384]{2,1,0:T(1,128)S(1)}, f32[16,1,384]{2,1,0:T(1,128)S(1)}, u32[]{:S(2)}, u32[]{:S(2)}) collective-permute-start(f32[16,1,384]{2,1,0:T(1,128)S(1)} %get-tuple-element.8), channel_id=1, source_target_pairs={{1,0},{2,1},{3,2},{5,4},{6,5},{7,6},{9,8},{10,9},{11,10},{13,12},{... | collective-permute-start | bytes 73736 | tf_op jit(solution)/shard_map/ppermute | solution.py:281
  295.9 1.9 collective-permute-start.1
  297.8 1.2 fusion.7
  299.0 1.1 fusion.13
  300.3 4.5 %collective-permute-start.3 = (f32[1,16,384]{2,1,0:T(8,128)S(1)}, f32[1,16,384]{2,1,0:T(8,128)S(1)}, u32[]{:S(2)}, u32[]{:S(2)}) collective-permute-start(f32[1,16,384]{2,1,0:T(8,128)S(1)} %get-tuple-element.12), channel_id=1, source_target_pairs={{4,0},{8,4},{12,8},{16,12},{20,16},{24,20},{28,24},{5,1},{9,5},{13... | collective-permute-start | bytes 73736 | tf_op jit(solution)/shard_map/ppermute | solution.py:281
  304.8 0.0 collective-permute-done.2
  304.8 4.0 %collective-permute-start.5 = (f32[16,1,384]{2,1,0:T(1,128)S(1)}, f32[16,1,384]{2,1,0:T(1,128)S(1)}, u32[]{:S(2)}, u32[]{:S(2)}) collective-permute-start(f32[16,1,384]{2,1,0:T(1,128)S(1)} %get-tuple-element.5), channel_id=1, source_target_pairs={{0,1},{1,2},{2,3},{4,5},{5,6},{6,7},{8,9},{9,10},{10,11},{12,13},{... | collective-permute-start | bytes 73736 | tf_op jit(solution)/shard_map/ppermute | solution.py:280
  308.8 1.9 collective-permute-start.7
  310.7 0.1 fusion.11
  310.8 3.7 %collective-permute-done.7 = f32[16,1,384]{2,1,0:T(1,128)S(1)} collective-permute-done((f32[16,1,384]{2,1,0:T(1,128)S(1)}, f32[16,1,384]{2,1,0:T(1,128)S(1)}, u32[]{:S(2)}, u32[]{:S(2)}) %collective-permute-start.7) | collective-permute-done | bytes 24608 | tf_op jit(solution)/shard_map/ppermute | solution.py:281
  314.5 2.2 fusion.3
  316.7 0.7 copy.24
  (15 shorter events, 0.1 us)
Async XLA Ops:
  6.4 289.5 %copy-start.1 = (f32[16,16,384]{2,1,0:T(8,128)S(1)}, f32[16,16,384]{2,1,0:T(8,128)}, u32[]{:S(2)}) copy-start(f32[16,16,384]{2,1,0:T(8,128)} %param.23) | copy-start | bytes 1179652
  279.8 36.9 %copy-start = (f32[256,384]{1,0:T(8,128)S(1)}, f32[256,384]{1,0:T(8,128)}, u32[]{:S(2)}) copy-start(f32[256,384]{1,0:T(8,128)} %shard_map.131) | copy-start | bytes 1179652
  280.6 19.6 %collective-permute-start = (f32[1,16,384]{2,1,0:T(8,128)S(1)}, f32[1,16,384]{2,1,0:T(8,128)S(1)}, u32[]{:S(2)}, u32[]{:S(2)}) collective-permute-start(f32[1,16,384]{2,1,0:T(8,128)S(1)} %get-tuple-element.17), channel_id=1, source_target_pairs={{0,4},{4,8},{8,12},{12,16},{16,20},{20,24},{24,28},{1,5},{5,9},{9,... | collective-permute-start | bytes 73736 | tf_op jit(solution)/shard_map/ppermute | solution.py:280
  283.1 21.7 %collective-permute-start.2 = (f32[1,16,384]{2,1,0:T(8,128)S(1)}, f32[1,16,384]{2,1,0:T(8,128)S(1)}, u32[]{:S(2)}, u32[]{:S(2)}) collective-permute-start(f32[1,16,384]{2,1,0:T(8,128)S(1)} %get-tuple-element.16), channel_id=1, source_target_pairs={{4,0},{8,4},{12,8},{16,12},{20,16},{24,20},{28,24},{5,1},{9,5},{13... | collective-permute-start | bytes 73736 | tf_op jit(solution)/shard_map/ppermute | solution.py:281
  288.1 20.6 %collective-permute-start.4 = (f32[16,1,384]{2,1,0:T(1,128)S(1)}, f32[16,1,384]{2,1,0:T(1,128)S(1)}, u32[]{:S(2)}, u32[]{:S(2)}) collective-permute-start(f32[16,1,384]{2,1,0:T(1,128)S(1)} %get-tuple-element.9), channel_id=1, source_target_pairs={{0,1},{1,2},{2,3},{4,5},{5,6},{6,7},{8,9},{9,10},{10,11},{12,13},{... | collective-permute-start | bytes 73736 | tf_op jit(solution)/shard_map/ppermute | solution.py:280
  291.7 19.0 %collective-permute-start.6 = (f32[16,1,384]{2,1,0:T(1,128)S(1)}, f32[16,1,384]{2,1,0:T(1,128)S(1)}, u32[]{:S(2)}, u32[]{:S(2)}) collective-permute-start(f32[16,1,384]{2,1,0:T(1,128)S(1)} %get-tuple-element.8), channel_id=1, source_target_pairs={{1,0},{2,1},{3,2},{5,4},{6,5},{7,6},{9,8},{10,9},{11,10},{13,12},{... | collective-permute-start | bytes 73736 | tf_op jit(solution)/shard_map/ppermute | solution.py:281
  295.9 14.9 %collective-permute-start.1 = (f32[1,16,384]{2,1,0:T(8,128)S(1)}, f32[1,16,384]{2,1,0:T(8,128)S(1)}, u32[]{:S(2)}, u32[]{:S(2)}) collective-permute-start(f32[1,16,384]{2,1,0:T(8,128)S(1)} %get-tuple-element.13), channel_id=1, source_target_pairs={{0,4},{4,8},{8,12},{12,16},{16,20},{20,24},{24,28},{1,5},{5,9},{9,... | collective-permute-start | bytes 73736 | tf_op jit(solution)/shard_map/ppermute | solution.py:280
  300.3 10.5 %collective-permute-start.3 = (f32[1,16,384]{2,1,0:T(8,128)S(1)}, f32[1,16,384]{2,1,0:T(8,128)S(1)}, u32[]{:S(2)}, u32[]{:S(2)}) collective-permute-start(f32[1,16,384]{2,1,0:T(8,128)S(1)} %get-tuple-element.12), channel_id=1, source_target_pairs={{4,0},{8,4},{12,8},{16,12},{20,16},{24,20},{28,24},{5,1},{9,5},{13... | collective-permute-start | bytes 73736 | tf_op jit(solution)/shard_map/ppermute | solution.py:281
  304.8 6.0 %collective-permute-start.5 = (f32[16,1,384]{2,1,0:T(1,128)S(1)}, f32[16,1,384]{2,1,0:T(1,128)S(1)}, u32[]{:S(2)}, u32[]{:S(2)}) collective-permute-start(f32[16,1,384]{2,1,0:T(1,128)S(1)} %get-tuple-element.5), channel_id=1, source_target_pairs={{0,1},{1,2},{2,3},{4,5},{5,6},{6,7},{8,9},{9,10},{10,11},{12,13},{... | collective-permute-start | bytes 73736 | tf_op jit(solution)/shard_map/ppermute | solution.py:280
  308.8 5.7 %collective-permute-start.7 = (f32[16,1,384]{2,1,0:T(1,128)S(1)}, f32[16,1,384]{2,1,0:T(1,128)S(1)}, u32[]{:S(2)}, u32[]{:S(2)}) collective-permute-start(f32[16,1,384]{2,1,0:T(1,128)S(1)} %get-tuple-element.4), channel_id=1, source_target_pairs={{1,0},{2,1},{3,2},{5,4},{6,5},{7,6},{9,8},{10,9},{11,10},{13,12},{... | collective-permute-start | bytes 73736 | tf_op jit(solution)/shard_map/ppermute | solution.py:281
